TPU v7x, 32 devices: a whole 2x2x4 slice. The times are simulated.
32 devices in a mesh: group: 2 (over x), feat: 8 (over z, y), layer: 2 (over core).
Axes of the slice: x: 2, y: 2, z: 4, core: 2. Of those that a mesh axis runs over, the one named last changes fastest.
Arguments:
- inputs: bfloat16 [2, 1024, 4096], P('layer', ('group', 'feat')), parts along dimension 1, may hold values from -6 to 6
- targets: bfloat16 [1024, 2, 4096], P(('group', 'feat'), None, 'layer'), parts along dimension 0, may hold values from -6 to 6
- tiles: int32 [2, 1024, 4], P('layer', 'group'), parts along dimension 1, may hold values from 0 to 127, as said below
- enc_weight: bfloat16 [2, 4096, 16384], P('layer', None, 'feat'), may hold values from -0.09375 to 0.09375
- enc_bias: bfloat16 [2, 16384], P('layer', 'feat'), may hold values from -3 to 3
- dec_weight: bfloat16 [2, 2, 16384, 4096], P('layer', None, 'feat'), may hold values from -0.25 to 0.25
- dec_bias: bfloat16 [2, 4096], P(None, 'layer'), may hold values from -3 to 3
Outputs:
- error: bfloat16 [1024, 2, 4096], P(('group', 'feat'), None, 'layer'), parts along dimension 0
There are 2 independent parts, one for each index of `group`. A program takes and returns all parts, laid end to end along the dimension named above; an argument that names none is the same for every part. Nothing has to cross between parts.
Inputs may be any that keep to these rules, and one draw needn't show every extreme that they name: Each row lists 4 different tiles that lie in 4 different feature blocks of 16 consecutive tiles; among the 64 consecutive tokens of one index of feat, at most 32 rows list a tile of any one block, and in every such token block and source layer some feature block is listed by exactly 32 rows.
All inputs are finite; a program needn't handle non-finite values.
Results may differ from a plain program's by a relative error of at most 0.0085.
Values may be sent and summed in bfloat16 or wider, within the bound.
A program may use at most 128 MiB of HBM per device.

v0:
```python
import jax
import jax.numpy as jnp
from jax import lax
from jax.sharding import PartitionSpec as P


def local(inputs, targets, tiles, enc_weight, enc_bias, dec_weight, dec_bias):
    source = lax.axis_index("layer")
    feat_index = lax.axis_index("feat")
    local_feats = enc_weight.shape[2]
    tiles_here = local_feats // 128
    tile_list = tiles[0] - feat_index * tiles_here
    tile_slots = jnp.arange(tiles_here, dtype=jnp.int32)
    weight_in = enc_weight[0]
    bias_in = enc_bias[0].astype(jnp.float32)
    target_count = dec_weight.shape[1]
    preact = (
        jnp.dot(
            lax.all_gather(inputs[0], "feat", axis=0, tiled=True),
            weight_in,
            preferred_element_type=jnp.float32,
        )
        + bias_in
    )
    active = jnp.any(tile_list[:, :, None] == tile_slots[None, None, :], axis=1)
    keep_mask = jnp.repeat(active, 128, axis=1)
    activations = jnp.where(keep_mask, jnp.maximum(preact, 0.0), 0.0).astype(jnp.bfloat16)
    columns = []
    for target in range(target_count):
        weight_out = dec_weight[0, target]
        product = jnp.dot(activations, weight_out, preferred_element_type=jnp.float32)
        product = product * (source <= target).astype(jnp.float32)
        columns.append(product)
    row_sums = lax.psum_scatter(
        jnp.stack(columns, axis=1).astype(jnp.bfloat16), "feat", scatter_dimension=0, tiled=True
    )
    summed = lax.psum_scatter(row_sums, "layer", scatter_dimension=2, tiled=True).astype(
        jnp.float32
    )
    result = summed + dec_bias.astype(jnp.float32)[None] - targets.astype(jnp.float32)
    return result.astype(jnp.bfloat16)


def solution(mesh):
    return jax.shard_map(
        local,
        mesh=mesh,
        in_specs=(
            P("layer", ("group", "feat"), None),
            P(("group", "feat"), None, "layer"),
            P("layer", "group", None),
            P("layer", None, "feat"),
            P("layer", "feat"),
            P("layer", None, "feat", None),
            P(None, "layer"),
        ),
        out_specs=P(("group", "feat"), None, "layer"),
        check_vma=False,
    )
```

profile of v0, /device:TPU:0, one launch (start us, length us, event | category | flops | bytes accessed | tf_op | source)
XLA Modules:
  0.0 302.1 jit_solution(17906146560824852788)
XLA Ops:
  6.5 0.0 all-gather.3.cloned.1.call-start
  6.5 0.7 all-gather.3.cloned.1.call-update
  7.3 0.0 reduce-scatter.3.cloned.1.call-start
  7.3 0.7 subtract_bitcast_fusion
  8.0 0.2 copy.11
  8.2 0.7 add.31
  8.9 76.7 %all-gather.3.cloned.1.call-done = bf16[1,512,4096]{2,1,0:T(8,128)(2,1)} async-done(((bf16[1,64,4096]{2,1,0:T(8,128)(2,1)}), bf16[1,512,4096]{2,1,0:T(8,128)(2,1)}) %all-gather.3.cloned.1.call-update) | async-done | bytes 4194320 | tf_op jit(solution)/shard_map/all_gather | solution.py:19
  85.6 3.4 %broadcast_in_dim.3 = pred[512,16,128]{2,1,0:T(8,128)(4,1)S(1)} broadcast(pred[512,16]{1,0:T(8,128)(4,1)S(1)} %copy.11), dimensions={0,1} | broadcast | bytes 1056768 | tf_op jit(solution)/shard_map/broadcast_in_dim | solution.py:26
  89.1 14.0 %select_convert_fusion = bf16[512,2048]{1,0:T(8,128)(2,1)S(1)} fusion(pred[64,8,16,128]{3,2,1,0:T(8,128)(4,1)S(1)} %bitcast.36, bf16[1,4096,2048]{2,1,0:T(8,128)(2,1)} %param.10, bf16[1,512,4096]{2,1,0:T(8,128)(2,1)} %all-gather.3.cloned.1.call-done, f32[2048]{0:T(1024)S(1)} %bitcast.37), kind=kOutput, calls=%fused_computation.14 | convolution fusion | flops 8594128896 | bytes 24125440 | tf_op jit(solution)/shard_map/dot_general | solution.py:18
  103.0 12.5 %fusion.12 = bf16[512,1,4096]{2,0,1:T(8,128)(2,1)S(1)} fusion(bf16[512,2048]{1,0:T(8,128)(2,1)S(1)} %select_convert_fusion, bf16[1,2,2048,4096]{3,2,1,0:T(8,128)(2,1)} %param.12, f32[]{:T(128)S(6)} %convert_element_type.25), kind=kOutput, calls=%fused_computation.11 | convolution fusion | flops 8594128896 | bytes 23068676 | tf_op jit(solution)/shard_map/dot_general | solution.py:31
  115.5 13.9 %fusion.15 = bf16[512,1,4096]{2,0,1:T(8,128)(2,1)} fusion(bf16[512,2048]{1,0:T(8,128)(2,1)S(1)} %select_convert_fusion, bf16[1,2,2048,4096]{3,2,1,0:T(8,128)(2,1)} %param.12, f32[]{:T(128)S(6)} %convert_element_type.26), kind=kOutput, calls=%fused_computation.12 | convolution fusion | flops 8594128896 | bytes 23068676 | tf_op jit(solution)/shard_map/dot_general | solution.py:31
  129.4 6.2 %pad_maximum_fusion = bf16[512,2,4096]{2,0,1:T(8,128)(2,1)} fusion(bf16[512,1,4096]{2,0,1:T(8,128)(2,1)} %fusion.15, bf16[512,1,4096]{2,0,1:T(8,128)(2,1)S(1)} %fusion.12), kind=kLoop, calls=%fused_computation.8 | loop fusion | flops 4194304 | bytes 16777216 | tf_op jit(solution)/shard_map/stack | solution.py:35
  135.5 0.0 copy-start.1
  135.6 0.0 copy-start
  135.6 0.0 reduce-scatter.3.cloned.1.call-update
  135.6 0.0 reduce-scatter.5.cloned.1.call-start
  135.6 147.4 %reduce-scatter.3.cloned.1.call-done = bf16[64,2,4096]{2,0,1:T(8,128)(2,1)} async-done(((bf16[512,2,4096]{2,0,1:T(8,128)(2,1)}), bf16[64,2,4096]{2,0,1:T(8,128)(2,1)}) %reduce-scatter.3.cloned.1.call-update) | async-done | bytes 1048592 | tf_op jit(solution)/shard_map/reduce_scatter | solution.py:34
  283.0 0.0 reduce-scatter.5.cloned.1.call-update
  283.0 0.0 copy-done.1
  283.1 9.8 %reduce-scatter.5.cloned.1.call-done = bf16[64,2,2048]{2,0,1:T(8,128)(2,1)} async-done(((bf16[64,2,4096]{2,0,1:T(8,128)(2,1)}), bf16[64,2,2048]{2,0,1:T(8,128)(2,1)}) %reduce-scatter.5.cloned.1.call-update) | async-done | bytes 524304 | tf_op jit(solution)/shard_map/reduce_scatter | solution.py:37
  292.9 0.0 copy-done
  292.9 1.3 subtract_convert_fusion
  294.2 1.3 copy.13
  (2 shorter events, 0.0 us)
Async XLA Ops:
  6.5 79.1 %all-gather.3.cloned.1.call-start = ((), (), s32[]{:S(2)}) async-start(), calls=%async_computation.4 | async-start | bytes 4718592 | tf_op jit(solution)/shard_map/all_gather | solution.py:19
  7.3 275.8 %reduce-scatter.3.cloned.1.call-start = ((), (), s32[]{:S(2)}) async-start(), calls=%async_computation.2 | async-start | bytes 9437184 | tf_op jit(solution)/shard_map/reduce_scatter | solution.py:34
  135.5 147.5 %copy-start.1 = (bf16[2,2048]{1,0:T(2,128)(2,1)S(1)}, bf16[2,2048]{1,0:T(2,128)(2,1)}, u32[]{:S(2)}) copy-start(bf16[2,2048]{1,0:T(2,128)(2,1)} %param.13) | copy-start | bytes 24580
  135.6 157.4 %copy-start = (bf16[64,2,2048]{2,1,0:T(2,128)(2,1)S(1)}, bf16[64,2,2048]{2,1,0:T(2,128)(2,1)}, u32[]{:S(2)}) copy-start(bf16[64,2,2048]{2,1,0:T(2,128)(2,1)} %param.8) | copy-start | bytes 1572868
  135.6 157.3 %reduce-scatter.5.cloned.1.call-start = ((), (), s32[]{:S(2)}) async-start(), calls=%async_computation.3 | async-start | bytes 1572864 | tf_op jit(solution)/shard_map/reduce_scatter | solution.py:37
Sparse Core Ops, SparseCore 0:
  9.5 76.0 all-gather.2
  135.7 147.2 reduce-scatter.2
  285.4 7.5 reduce-scatter.4
where the time goes:
time: 302 us
  waiting for transfers between devices  235 us (78%)
  matrix products  40.3 us (13%)
  between operations  13.2 us (4%)
  other arithmetic  8.9 us (3%)
  local copies, waits for them, and re-layouts  4.95 us (2%)
    reduce_scatter x1, waiting for transfers between devices, local(): lax.psum_scatter(jnp.stack(columns, axis=1).astype(jnp.bfloat16), 'feat',...  147 us
    all_gather x1, waiting for transfers between devices, local(): lax.all_gather(inputs[0], 'feat', axis=0, tiled=True)  76.7 us
    dot_general x2, matrix products, local(): jnp.dot(activations, weight_out, preferred_element_type=jnp.float32)  26.3 us
    dot_general x1, matrix products, local(): jnp.dot(lax.all_gather(inputs[0], 'feat', axis=0, tiled=True), weight_in,...  14 us
    reduce_scatter x1, waiting for transfers between devices, local(): lax.psum_scatter(row_sums, 'layer', scatter_dimension=2, tiled=True)  9.84 us
    another operation x1, other arithmetic, local(): jnp.stack(columns, axis=1).astype(jnp.bfloat16)  6.18 us
  transfers between devices with their start and end apart: 3, of which 3 were waited for; matrix products, arithmetic and copies ran while one was open for 1% of the time, Pallas kernels for 0%

commit v1 on v0

v1 whole, which is shorter than its diff:
```python
import functools

import jax
import jax.numpy as jnp
from jax import lax
from jax.experimental import pallas as pl
from jax.experimental.pallas import tpu as pltpu
from jax.sharding import PartitionSpec as P

MESH = pl.DeviceIdType.MESH
NY = 2
NK = 4
NJ = 4
BF = jnp.bfloat16
F32 = jnp.float32


def kernel(cfg, tt_ref, x_ref, bias_ref, we_ref, wd_ref, out_ref,
           wbuf, xcol, xp, ysend, acc, act, ppbuf, mbuf, cbuf, obuf, zacc, zown,
           w_sem, g_send, g_recv, y_send, y_recv, pp_send, pp_recv,
           e_send, e_recv, z_send, z_recv, o_recv):
    nz, tok, cap, th, width, feats = cfg
    f = lax.axis_index("feat")
    s = lax.axis_index("layer")
    z = lax.div(f, NY)
    y = lax.rem(f, NY)
    o = 1 - s
    f_par = z * NY + (1 - y)
    has_lo = z > 0
    has_hi = z < nz - 1
    kc = width // NK
    half = width // 2
    jc = half // NJ
    rows = nz * cap
    fh = feats // 2

    def w_copies(p, slot):
        if p < NK:
            return [pltpu.make_async_copy(
                we_ref.at[0, pl.ds(p * kc, kc), pl.ds(i * fh, fh)],
                wbuf.at[slot, pl.ds(i * kc, kc), :], w_sem.at[p, i]) for i in range(2)]
        j, t = (p - NK) // 2, (p - NK) % 2
        return [pltpu.make_async_copy(
            wd_ref.at[0, t, :, pl.ds(pl.multiple_of(h * half + j * jc, jc), jc)],
            wbuf.at[slot, :, pl.ds(i * jc, jc)], w_sem.at[p, i]) for i, h in enumerate((s, o))]

    def w_start(p):
        def go():
            for c in w_copies(p, p % 8):
                c.start()
        if p >= NK and (p - NK) % 2 == 0:
            pl.when(s == 0)(go)
        else:
            go()

    def w_wait(p):
        for c in w_copies(p, p % 8):
            c.wait()

    barrier = pltpu.get_barrier_semaphore()
    lo_id = {"feat": jnp.maximum(f - NY, 0)}
    hi_id = {"feat": jnp.minimum(f + NY, nz * NY - 1)}
    par_id = {"feat": f_par}
    core_id = {"layer": o}
    diag_id = {"feat": f_par, "layer": o}

    def greet(dev):
        pl.semaphore_signal(barrier, inc=1, device_id=dev, device_id_type=MESH)

    for dev in (par_id, core_id, diag_id):
        greet(dev)
    pl.when(has_lo)(lambda: greet(lo_id))
    pl.when(has_hi)(lambda: greet(hi_id))
    for p in range(8):
        w_start(p)
    pl.semaphore_wait(barrier, 3 + has_lo.astype(jnp.int32) + has_hi.astype(jnp.int32))

    def remote(src, dst, ss, rs, dev):
        return pltpu.make_async_remote_copy(
            src_ref=src, dst_ref=dst, send_sem=ss, recv_sem=rs,
            device_id=dev, device_id_type=MESH)

    def kcols(k):
        return pl.ds(pl.multiple_of(k * kc, kc), kc)

    def g_copy(src, zc, k, direction, dev):
        return remote(src.at[:, kcols(k)], xcol.at[zc, :, kcols(k)],
                      g_send.at[direction, zc, k], g_recv.at[zc, k], dev)

    for k in range(NK):
        pl.when(has_hi)(lambda: g_copy(x_ref, z, k, 0, hi_id).start())
        pl.when(has_lo)(lambda: g_copy(x_ref, z, k, 1, lo_id).start())

    blk = lax.div(tt_ref[...], th)
    ri = lax.broadcasted_iota(jnp.int32, (cap, 128), 0).astype(F32)
    tri = (lax.broadcasted_iota(jnp.int32, (128, 128), 0)
           <= lax.broadcasted_iota(jnp.int32, (128, 128), 1)).astype(F32)

    def picks(b, count):
        on = jnp.max(jnp.where(blk == b, 1.0, 0.0), axis=1)
        rank = jnp.dot(on, tri, preferred_element_type=F32) - 1.0
        return [jnp.where((ri == rank[q:q + 1]) & (on[q:q + 1] > 0.5), 1.0, 0.0).astype(BF)
                for q in range(count)]

    own = picks(f, nz * NY)
    par = picks(f_par, nz)
    for q in range(nz):
        ppbuf[0, q, 0:cap, :] = own[q]
        ppbuf[0, q, cap:2 * cap, :] = par[q]
    pp_copy = remote(ppbuf.at[0], ppbuf.at[1], pp_send, pp_recv, core_id)
    pp_copy.start()
    ti = lax.broadcasted_iota(jnp.int32, (th, 128), 0) + f * th
    for q in range(nz * NY):
        hit = jnp.zeros((th, 128), F32)
        for c in range(tt_ref.shape[1]):
            hit = jnp.where(tt_ref[q, c:c + 1, :] == ti, 1.0, hit)
        mbuf[q * cap:(q + 1) * cap, :] = lax.dot_general(
            own[q], hit.astype(BF), (((1,), (1,)), ((), ())), preferred_element_type=F32)
    acc[...] = jnp.broadcast_to(bias_ref[...].astype(F32), acc.shape)
    zero = jnp.zeros((rows, jc), BF)
    for i in range(2):
        for j in range(NJ):
            cbuf[2 * (1 - s) + i, j, 0] = zero

    def y_copy(zc, k):
        r = pl.ds(pl.multiple_of(rows + zc * cap, cap), cap)
        return remote(ysend.at[zc, :, kcols(k)], xp.at[r, kcols(k)],
                      y_send.at[zc, k], y_recv.at[zc, k], par_id)

    def pack(src, zc, k):
        v = jnp.dot(ppbuf[0, zc, :, 0:tok], src[:, kcols(k)],
                    preferred_element_type=F32).astype(BF)
        ysend[zc, :, kcols(k)] = v[cap:]
        y_copy(zc, k).start()
        xp[pl.ds(pl.multiple_of(zc * cap, cap), cap), kcols(k)] = v[:cap]

    def over_k(fn):
        def body(k, c):
            fn(k)
            return c
        lax.fori_loop(0, NK, body, 0)

    over_k(lambda k: pack(x_ref, z, k))

    for dist in range(1, nz):
        def step(k):
            def arrive(zc, direction, more, dev):
                g_copy(x_ref, zc, k, direction, dev).wait_recv()
                pl.when(more)(lambda: g_copy(xcol.at[zc], zc, k, direction, dev).start())
                pack(xcol.at[zc], zc, k)
            pl.when(z >= dist)(lambda: arrive(z - dist, 0, has_hi, hi_id))
            pl.when(z + dist < nz)(lambda: arrive(z + dist, 1, has_lo, lo_id))
        over_k(step)

    for k in range(NK):
        w_wait(k)
        for zc in range(nz):
            y_copy(zc, k).wait_recv()
        for i in range(2):
            def enc(n, c):
                dst = pl.ds(pl.multiple_of(i * fh + n * 256, 256), 256)
                acc[:, dst] += jnp.dot(
                    xp[:, k * kc:(k + 1) * kc],
                    wbuf[k, i * kc:(i + 1) * kc, pl.ds(pl.multiple_of(n * 256, 256), 256)],
                    preferred_element_type=F32)
                return c
            lax.fori_loop(0, fh // 256, enc, 0)
    for p in range(8, NK + 2 * NJ):
        w_start(p)
    for i in range(th):
        c = slice(i * 128, (i + 1) * 128)
        act[:, c] = jnp.where(mbuf[:, i:i + 1] > 0.5, jnp.maximum(acc[:, c], 0.0), 0.0).astype(BF)

    pp_copy.wait()
    ex = ((0, par_id), (1, core_id), (2, diag_id))

    def e_copy(m, dev, j, t):
        return remote(obuf.at[m, j, t], cbuf.at[m + 1, j, t],
                      e_send.at[m, j, t], e_recv.at[m, j, t], dev)

    def decode(j):
        for t in range(2):
            def go():
                p = NK + 2 * j + t
                w_wait(p)
                for h in range(2):
                    for n in range(jc // 256):
                        v = jnp.dot(act[...], wbuf[p % 8, :, h * jc + n * 256:h * jc + (n + 1) * 256],
                                    preferred_element_type=F32).astype(BF)
                        c = slice(n * 256, (n + 1) * 256)
                        if h == 0:
                            cbuf[0, j, t, :, c] = v[:rows]
                            obuf[0, j, t, :, c] = v[rows:]
                        else:
                            obuf[1, j, t, :, c] = v[:rows]
                            obuf[2, j, t, :, c] = v[rows:]
                for m, dev in ex:
                    e_copy(m, dev, j, t).start()
            if t == 0:
                pl.when(s == 0)(go)
            else:
                go()

    def part(d, j, t):
        sel = ppbuf[:, d, :, 0:tok].reshape(4 * cap, tok)
        r = pl.ds(pl.multiple_of(d * cap, cap), cap)
        v = cbuf[:, j, t, r, :].reshape(4 * cap, jc)
        return lax.dot_general(sel, v, (((0,), (0,)), ((), ())), preferred_element_type=F32)

    def z_copy(d, j, down, dev, last):
        dst = zown.at[j] if last else zacc.at[d, j]
        return remote(zacc.at[d, j], dst, z_send.at[d, j],
                      o_recv.at[j] if last else z_recv.at[d, j], dev)

    def line(j):
        for m, dev in ex:
            e_copy(m, dev, j, 1).wait_recv()
        pl.when(s == 0)(lambda: e_copy(0, par_id, j, 0).wait_recv())

        def others():
            e_copy(1, core_id, j, 0).wait_recv()
            e_copy(2, diag_id, j, 0).wait_recv()
        pl.when(s == 1)(others)
        for dist in range(nz - 1, 0, -1):
            def run(d, down, has_in, dev, in_dev):
                vs = [part(d, j, t) for t in range(2)]

                def first():
                    for t in range(2):
                        zacc[d, j, t] = vs[t].astype(BF)

                def add():
                    z_copy(d, j, down, in_dev, False).wait_recv()
                    for t in range(2):
                        zacc[d, j, t] = (vs[t] + zacc[d, j, t].astype(F32)).astype(BF)
                pl.when(has_in)(add)
                pl.when(jnp.logical_not(has_in))(first)
                z_copy(d, j, down, dev, down and dist == 1).start()
            pl.when(z >= dist)(lambda: run(z - dist, True, has_hi, lo_id, hi_id))
            pl.when(z + dist < nz)(lambda: run(z + dist, False, has_lo, hi_id, lo_id))

    decode(0)
    decode(1)
    for j in range(NJ):
        line(j)
        if j + 2 < NJ:
            decode(j + 2)
    for j in range(NJ):
        c = slice(j * jc, (j + 1) * jc)
        for t in range(2):
            out_ref[t, :, c] = part(z, j, t)

        def below():
            z_copy(z, j, False, lo_id, False).wait_recv()
            for t in range(2):
                out_ref[t, :, c] += zacc[z, j, t].astype(F32)

        def above():
            z_copy(z, j, True, hi_id, True).wait_recv()
            for t in range(2):
                out_ref[t, :, c] += zown[j, t].astype(F32)
        pl.when(has_lo)(below)
        pl.when(has_hi)(above)

    def sent(k):
        def up(zc):
            g_copy(x_ref, zc, k, 0, hi_id).wait_send()

        def down(zc):
            g_copy(x_ref, zc, k, 1, lo_id).wait_send()
        for zc in range(nz):
            pl.when(has_hi & (zc <= z))(lambda: up(zc))
            pl.when(has_lo & (zc >= z))(lambda: down(zc))
            y_copy(zc, k).wait_send()
    over_k(sent)
    for j in range(NJ):
        for m, dev in ex:
            e_copy(m, dev, j, 1).wait_send()

        def zero_t():
            for m, dev in ex:
                e_copy(m, dev, j, 0).wait_send()
        pl.when(s == 0)(zero_t)
        for d in range(nz):
            pl.when(z != d)(lambda: z_copy(d, j, True, lo_id, False).wait_send())


def fused(tt, x, bias, we, wd, nz):
    tok, width = x.shape
    feats = we.shape[2]
    th = feats // 128
    cap = tok * tt.shape[1] // (nz * NY)
    rows = nz * cap
    kc = width // NK
    jc = width // 2 // NJ
    dma = pltpu.SemaphoreType.DMA
    vmem = pl.BlockSpec(memory_space=pltpu.VMEM)
    hbm = pl.BlockSpec(memory_space=pl.ANY)
    return pl.pallas_call(
        functools.partial(kernel, (nz, tok, cap, th, width, feats)),
        out_shape=jax.ShapeDtypeStruct((2, tok, width // 2), F32),
        in_specs=[vmem, vmem, vmem, hbm, hbm],
        out_specs=vmem,
        scratch_shapes=[
            pltpu.VMEM((8, 2 * kc, feats // 2), BF),
            pltpu.VMEM((nz, tok, width), BF),
            pltpu.VMEM((2 * rows, width), BF),
            pltpu.VMEM((nz, cap, width), BF),
            pltpu.VMEM((2 * rows, feats), F32),
            pltpu.VMEM((2 * rows, feats), BF),
            pltpu.VMEM((2, nz, 2 * cap, 128), BF),
            pltpu.VMEM((2 * rows, th), F32),
            pltpu.VMEM((4, NJ, 2, rows, jc), BF),
            pltpu.VMEM((3, NJ, 2, rows, jc), BF),
            pltpu.VMEM((nz, NJ, 2, tok, jc), BF),
            pltpu.VMEM((NJ, 2, tok, jc), BF),
            dma((NK + 2 * NJ, 2)),
            dma((2, nz, NK)), dma((nz, NK)),
            dma((nz, NK)), dma((nz, NK)),
            dma, dma,
            dma((3, NJ, 2)), dma((3, NJ, 2)),
            dma((nz, NJ)), dma((nz, NJ)), dma((NJ,)),
        ],
        compiler_params=pltpu.CompilerParams(
            collective_id=0, has_side_effects=True, vmem_limit_bytes=58 * 2**20),
        cost_estimate=pl.CostEstimate(
            flops=2 * 2 * rows * feats * width * 3, bytes_accessed=48 * 2**20, transcendentals=0),
    )(tt, x, bias, we, wd)


def local_line(inputs, targets, tiles, enc_weight, enc_bias, dec_weight, dec_bias, *, nz):
    y = lax.axis_index("feat") % NY
    tok = inputs.shape[1]
    kt = tiles.shape[2]
    tt = tiles[0].T.reshape(kt, nz, NY, tok).transpose(2, 1, 0, 3)
    tt = jnp.where(y == 0, tt, tt[::-1]).reshape(nz * NY, kt, tok)
    tt = jnp.pad(tt, ((0, 0), (0, 0), (0, 128 - tok)), constant_values=-4096)
    recon = fused(tt, inputs[0], enc_bias, enc_weight, dec_weight, nz)
    result = (recon.transpose(1, 0, 2) + dec_bias.astype(F32)[None]
              - targets.astype(F32))
    return result.astype(BF)


def local_any(inputs, targets, tiles, enc_weight, enc_bias, dec_weight, dec_bias):
    source = lax.axis_index("layer")
    feat_index = lax.axis_index("feat")
    th = enc_weight.shape[2] // 128
    x = lax.all_gather(inputs[0], "feat", axis=0, tiled=True)
    pre = jnp.dot(x, enc_weight[0], preferred_element_type=F32) + enc_bias[0].astype(F32)
    ids = feat_index * th + jnp.arange(th, dtype=jnp.int32)
    active = jnp.any(tiles[0][:, :, None] == ids[None, None, :], axis=1)
    act = jnp.where(jnp.repeat(active, 128, axis=1), jnp.maximum(pre, 0.0), 0.0).astype(BF)
    columns = []
    for target in range(dec_weight.shape[1]):
        product = jnp.dot(act, dec_weight[0, target], preferred_element_type=F32)
        columns.append(product * (source <= target).astype(F32))
    both = jnp.stack(columns, axis=1).astype(BF)
    halves = lax.psum_scatter(both, "layer", scatter_dimension=2, tiled=True)
    summed = lax.psum_scatter(halves, "feat", scatter_dimension=0, tiled=True).astype(F32)
    result = summed + dec_bias.astype(F32)[None] - targets.astype(F32)
    return result.astype(BF)


def solution(mesh):
    nf = mesh.shape["feat"]
    local = functools.partial(local_line, nz=nf // NY) if nf == 8 else local_any
    return jax.shard_map(
        local,
        mesh=mesh,
        in_specs=(
            P("layer", ("group", "feat"), None),
            P(("group", "feat"), None, "layer"),
            P("layer", "group", None),
            P("layer", None, "feat"),
            P("layer", "feat"),
            P("layer", None, "feat", None),
            P(None, "layer"),
        ),
        out_specs=P(("group", "feat"), None, "layer"),
        check_vma=False,
    )
```

time: 302 us -> 112 us (0.37)
  waiting for transfers between devices: 235 us -> 0 us
  Pallas kernels: 0 us -> 107 us
  matrix products: 40.3 us -> 0 us
  between operations: 13.2 us -> 0.03 us
  other arithmetic: 8.9 us -> 2.19 us
    reduce_scatter x2 -> x0, waiting for transfers between devices: 157 us -> none  [the longest x1 147 us: local(): lax.psum_scatter(jnp.stack(columns, axis=1).astype(jnp.bfloat16), 'feat',...]
    pallas_call x0 -> x1, Pallas kernels: none -> 107 us  [fused(): pl.pallas_call(functools.partial(kernel, (nz, tok, cap, th, width, feats)...]
    all_gather x1 -> x0, waiting for transfers between devices: 76.7 us -> none  [local(): lax.all_gather(inputs[0], 'feat', axis=0, tiled=True)]
    dot_general x3 -> x0, matrix products: 40.3 us -> none  [the longest x2 26.3 us: local(): jnp.dot(activations, weight_out, preferred_element_type=jnp.float32)]
    another operation x1 -> x0, other arithmetic: 6.18 us -> none  [local(): jnp.stack(columns, axis=1).astype(jnp.bfloat16)]
    broadcast_in_dim x1 -> x0, local copies, waits for them, and re-layouts: 3.44 us -> none  [local(): keep_mask = jnp.repeat(active, 128, axis=1)]
  transfers between devices with their start and end apart: 3 -> 0, of which waited for: 3 -> 0; matrix products, arithmetic and copies ran while one was open for 1% -> 0% of each run, Pallas kernels for 0% -> 0%
where the time goes in v1:
time: 112 us
  Pallas kernels  107 us (96%)
  local copies, waits for them, and re-layouts  2.8 us (2%)
  other arithmetic  2.19 us (2%)
    pallas_call x1, Pallas kernels, fused(): pl.pallas_call(functools.partial(kernel, (nz, tok, cap, th, width, feats)...  107 us

profile of v1, /device:TPU:0, one launch (start us, length us, event | category | flops | bytes accessed | tf_op | source)
XLA Modules:
  0.0 111.9 jit_solution(4772706467309730703)
XLA Ops:
  0.0 0.0 copy-start
  0.0 0.8 reshape.7
  0.9 0.6 pad.4.tt_ref
  1.5 0.7 convert_element_type.9
  2.2 106.9 %shard_map.73 = f32[2,64,2048]{2,1,0:T(8,128)} custom-call(s32[8,4,128]{2,1,0:T(4,128)} %pad.4.tt_ref, bf16[64,4096]{1,0:T(8,128)(2,1)} %bitcast.12, bf16[1,2048]{1,0:T(2,128)(2,1)} %bias_ref.1, bf16[1,4096,2048]{2,1,0:T(8,128)(2,1)} %we_ref.1, bf16[1,2,2048,4096]{3,2,1,0:T(8,128)(2,1)} %wd_ref.1), custom_call_target="tpu_custom_call" | custom-call | flops 12884901888 | bytes 50331648 | tf_op jit(solution)/shard_map/pallas_call | solution.py:299
  109.1 0.0 copy-done
  109.1 1.5 %fusion = bf16[64,2,2048]{2,0,1:T(8,128)(2,1)S(1)} fusion(f32[2,64,2048]{2,1,0:T(8,128)} %shard_map.73, bf16[64,2,2048]{2,1,0:T(2,128)(2,1)S(1)} %copy-done, f32[2,2048]{1,0:T(2,128)S(1)} %convert_element_type.9), kind=kLoop, calls=%fused_computation.1 | loop fusion | flops 1048576 | bytes 2113536 | tf_op jit(solution)/shard_map/convert_element_type | solution.py:341
  110.6 1.3 %copy.10 = bf16[64,2,2048]{2,1,0:T(2,128)(2,1)} copy(bf16[64,2,2048]{2,0,1:T(8,128)(2,1)S(1)} %fusion) | data formatting | bytes 1048576 | tf_op jit(solution)/shard_map/convert_element_type | solution.py:341
  (2 shorter events, 0.0 us)
Async XLA Ops:
  0.0 109.1 %copy-start = (bf16[64,2,2048]{2,1,0:T(2,128)(2,1)S(1)}, bf16[64,2,2048]{2,1,0:T(2,128)(2,1)}, u32[]{:S(2)}) copy-start(bf16[64,2,2048]{2,1,0:T(2,128)(2,1)} %param.8) | copy-start | bytes 1572868

commit v2 on v1

--- a/solution.py
+++ b/solution.py
@@ -11,12 +11,15 @@
 NY = 2
 NK = 4
 NJ = 4
+AHEAD = 3
+NE = 4
+ND = 4
 BF = jnp.bfloat16
 F32 = jnp.float32
 
 
 def kernel(cfg, tt_ref, x_ref, bias_ref, we_ref, wd_ref, out_ref,
-           wbuf, xcol, xp, ysend, acc, act, ppbuf, mbuf, cbuf, obuf, zacc, zown,
+           wbuf, ttbuf, xcol, xp, ysend, acc, act, ppbuf, mbuf, cbuf, obuf, zacc, zown,
            w_sem, g_send, g_recv, y_send, y_recv, pp_send, pp_recv,
            e_send, e_recv, z_send, z_recv, o_recv):
     nz, tok, cap, th, width, feats = cfg
@@ -34,21 +37,25 @@
     rows = nz * cap
     fh = feats // 2
 
+    ke = width // NE
+    per = NJ // ND
+
     def w_copies(p, slot):
-        if p < NK:
+        if p < NE:
             return [pltpu.make_async_copy(
-                we_ref.at[0, pl.ds(p * kc, kc), pl.ds(i * fh, fh)],
-                wbuf.at[slot, pl.ds(i * kc, kc), :], w_sem.at[p, i]) for i in range(2)]
-        j, t = (p - NK) // 2, (p - NK) % 2
+                we_ref.at[0, pl.ds(p * ke, ke), pl.ds(i * fh, fh)],
+                wbuf.at[slot, pl.ds(i * ke, ke), :], w_sem.at[p, i]) for i in range(2)]
+        jw, t = (p - NE) // 2, (p - NE) % 2
         return [pltpu.make_async_copy(
-            wd_ref.at[0, t, :, pl.ds(pl.multiple_of(h * half + j * jc, jc), jc)],
-            wbuf.at[slot, :, pl.ds(i * jc, jc)], w_sem.at[p, i]) for i, h in enumerate((s, o))]
+            wd_ref.at[0, t, :, pl.ds(pl.multiple_of(h * half + (jw * per + m) * jc, jc), jc)],
+            wbuf.at[slot, :, pl.ds((2 * m + i) * jc, jc)], w_sem.at[p, 2 * m + i])
+            for m in range(per) for i, h in enumerate((s, o))]
 
     def w_start(p):
         def go():
             for c in w_copies(p, p % 8):
                 c.start()
-        if p >= NK and (p - NK) % 2 == 0:
+        if p >= NE and (p - NE) % 2 == 0:
             pl.when(s == 0)(go)
         else:
             go()
@@ -91,7 +98,14 @@
         pl.when(has_hi)(lambda: g_copy(x_ref, z, k, 0, hi_id).start())
         pl.when(has_lo)(lambda: g_copy(x_ref, z, k, 1, lo_id).start())
 
-    blk = lax.div(tt_ref[...], th)
+    lane = lax.broadcasted_iota(jnp.int32, (tt_ref.shape[0], 128), 1)
+    for zc in range(nz):
+        t2 = tt_ref[:, zc * 128:(zc + 1) * 128]
+        swapped = pltpu.roll(t2, 64, 1)
+        ttbuf[zc] = jnp.where(lane < tok, jnp.where(y == 0, t2, swapped), -4096)
+        ttbuf[nz + zc] = jnp.where(lane < tok, jnp.where(y == 0, swapped, t2), -4096)
+
+    blk = lax.div(ttbuf[...], th)
     ri = lax.broadcasted_iota(jnp.int32, (cap, 128), 0).astype(F32)
     tri = (lax.broadcasted_iota(jnp.int32, (128, 128), 0)
            <= lax.broadcasted_iota(jnp.int32, (128, 128), 1)).astype(F32)
@@ -112,8 +126,8 @@
     ti = lax.broadcasted_iota(jnp.int32, (th, 128), 0) + f * th
     for q in range(nz * NY):
         hit = jnp.zeros((th, 128), F32)
-        for c in range(tt_ref.shape[1]):
-            hit = jnp.where(tt_ref[q, c:c + 1, :] == ti, 1.0, hit)
+        for c in range(tt_ref.shape[0]):
+            hit = jnp.where(ttbuf[q, c:c + 1, :] == ti, 1.0, hit)
         mbuf[q * cap:(q + 1) * cap, :] = lax.dot_general(
             own[q], hit.astype(BF), (((1,), (1,)), ((), ())), preferred_element_type=F32)
     acc[...] = jnp.broadcast_to(bias_ref[...].astype(F32), acc.shape)
@@ -150,22 +164,31 @@
                 pack(xcol.at[zc], zc, k)
             pl.when(z >= dist)(lambda: arrive(z - dist, 0, has_hi, hi_id))
             pl.when(z + dist < nz)(lambda: arrive(z + dist, 1, has_lo, lo_id))
-        over_k(step)
-
-    for k in range(NK):
-        w_wait(k)
-        for zc in range(nz):
-            y_copy(zc, k).wait_recv()
+        if dist < nz - 1:
+            over_k(step)
+
+    def encode(e):
+        w_wait(e)
+        for k in range(e * NK // NE, (e + 1) * NK // NE):
+            for zc in range(nz):
+                y_copy(zc, k).wait_recv()
         for i in range(2):
             def enc(n, c):
-                dst = pl.ds(pl.multiple_of(i * fh + n * 256, 256), 256)
+                dst = pl.ds(pl.multiple_of(i * fh + n * 512, 512), 512)
                 acc[:, dst] += jnp.dot(
-                    xp[:, k * kc:(k + 1) * kc],
-                    wbuf[k, i * kc:(i + 1) * kc, pl.ds(pl.multiple_of(n * 256, 256), 256)],
+                    xp[:, e * ke:(e + 1) * ke],
+                    wbuf[e, i * ke:(i + 1) * ke, pl.ds(pl.multiple_of(n * 512, 512), 512)],
                     preferred_element_type=F32)
                 return c
-            lax.fori_loop(0, fh // 256, enc, 0)
-    for p in range(8, NK + 2 * NJ):
+            lax.fori_loop(0, fh // 512, enc, 0)
+
+    pk = NK // NE
+    for k in range(NK):
+        step(k)
+        if k >= pk and k % pk == 0:
+            encode(k // pk - 1)
+    encode(NE - 1)
+    for p in range(8, NE + 2 * ND):
         w_start(p)
     for i in range(th):
         c = slice(i * 128, (i + 1) * 128)
@@ -181,19 +204,16 @@
     def decode(j):
         for t in range(2):
             def go():
-                p = NK + 2 * j + t
-                w_wait(p)
-                for h in range(2):
-                    for n in range(jc // 256):
-                        v = jnp.dot(act[...], wbuf[p % 8, :, h * jc + n * 256:h * jc + (n + 1) * 256],
-                                    preferred_element_type=F32).astype(BF)
-                        c = slice(n * 256, (n + 1) * 256)
-                        if h == 0:
-                            cbuf[0, j, t, :, c] = v[:rows]
-                            obuf[0, j, t, :, c] = v[rows:]
-                        else:
-                            obuf[1, j, t, :, c] = v[:rows]
-                            obuf[2, j, t, :, c] = v[rows:]
+                p = NE + 2 * (j // per) + t
+                if j % per == 0:
+                    w_wait(p)
+                m0 = j % per * 2 * jc
+                v = jnp.dot(act[...], wbuf[p % 8, :, m0:m0 + 2 * jc],
+                            preferred_element_type=F32).astype(BF)
+                cbuf[0, j, t] = v[:rows, :jc]
+                obuf[0, j, t] = v[rows:, :jc]
+                obuf[1, j, t] = v[:rows, jc:]
+                obuf[2, j, t] = v[rows:, jc:]
                 for m, dev in ex:
                     e_copy(m, dev, j, t).start()
             if t == 0:
@@ -239,12 +259,12 @@
             pl.when(z >= dist)(lambda: run(z - dist, True, has_hi, lo_id, hi_id))
             pl.when(z + dist < nz)(lambda: run(z + dist, False, has_lo, hi_id, lo_id))
 
-    decode(0)
-    decode(1)
+    for j in range(AHEAD):
+        decode(j)
     for j in range(NJ):
         line(j)
-        if j + 2 < NJ:
-            decode(j + 2)
+        if j + AHEAD < NJ:
+            decode(j + AHEAD)
     for j in range(NJ):
         c = slice(j * jc, (j + 1) * jc)
         for t in range(2):
@@ -289,9 +309,8 @@
     tok, width = x.shape
     feats = we.shape[2]
     th = feats // 128
-    cap = tok * tt.shape[1] // (nz * NY)
+    cap = tok * tt.shape[0] // (nz * NY)
     rows = nz * cap
-    kc = width // NK
     jc = width // 2 // NJ
     dma = pltpu.SemaphoreType.DMA
     vmem = pl.BlockSpec(memory_space=pltpu.VMEM)
@@ -302,7 +321,8 @@
         in_specs=[vmem, vmem, vmem, hbm, hbm],
         out_specs=vmem,
         scratch_shapes=[
-            pltpu.VMEM((8, 2 * kc, feats // 2), BF),
+            pltpu.VMEM((8, 2 * (width // NE), feats // 2), BF),
+            pltpu.VMEM((nz * NY, tt.shape[0], 128), jnp.int32),
             pltpu.VMEM((nz, tok, width), BF),
             pltpu.VMEM((2 * rows, width), BF),
             pltpu.VMEM((nz, cap, width), BF),
@@ -314,7 +334,7 @@
             pltpu.VMEM((3, NJ, 2, rows, jc), BF),
             pltpu.VMEM((nz, NJ, 2, tok, jc), BF),
             pltpu.VMEM((NJ, 2, tok, jc), BF),
-            dma((NK + 2 * NJ, 2)),
+            dma((NE + 2 * ND, 2 * NJ // ND)),
             dma((2, nz, NK)), dma((nz, NK)),
             dma((nz, NK)), dma((nz, NK)),
             dma, dma,
@@ -329,12 +349,7 @@
 
 
 def local_line(inputs, targets, tiles, enc_weight, enc_bias, dec_weight, dec_bias, *, nz):
-    y = lax.axis_index("feat") % NY
-    tok = inputs.shape[1]
-    kt = tiles.shape[2]
-    tt = tiles[0].T.reshape(kt, nz, NY, tok).transpose(2, 1, 0, 3)
-    tt = jnp.where(y == 0, tt, tt[::-1]).reshape(nz * NY, kt, tok)
-    tt = jnp.pad(tt, ((0, 0), (0, 0), (0, 128 - tok)), constant_values=-4096)
+    tt = tiles[0].T
     recon = fused(tt, inputs[0], enc_bias, enc_weight, dec_weight, nz)
     result = (recon.transpose(1, 0, 2) + dec_bias.astype(F32)[None]
               - targets.astype(F32))

time: 112 us -> 106 us (0.946); the launches traced: 112 us -> 104 us
  Pallas kernels: 107 us -> 101 us
  local copies, waits for them, and re-layouts: 2.8 us -> 1.34 us
    pallas_call x1, Pallas kernels: 107 us -> 101 us  [fused(): pl.pallas_call(functools.partial(kernel, (nz, tok, cap, th, width, feats)...]
where the time goes in v2:
time: 106 us; the launch traced here: 104 us
  Pallas kernels  101 us (95%)
  other arithmetic  2.24 us (2%)
  local copies, waits for them, and re-layouts  1.34 us (1%)
    pallas_call x1, Pallas kernels, fused(): pl.pallas_call(functools.partial(kernel, (nz, tok, cap, th, width, feats)...  101 us

profile of v2, /device:TPU:0, one launch (start us, length us, event | category | flops | bytes accessed | tf_op | source)
XLA Modules:
  0.0 104.2 jit_solution(9640433174880999259)
XLA Ops:
  0.0 0.0 copy-start
  0.0 0.8 convert_element_type.9
  0.8 100.6 %shard_map.73 = f32[2,64,2048]{2,1,0:T(8,128)} custom-call(s32[4,512]{1,0:T(4,128)} %bitcast.9, bf16[64,4096]{1,0:T(8,128)(2,1)} %bitcast.8, bf16[1,2048]{1,0:T(2,128)(2,1)} %bias_ref.1, bf16[1,4096,2048]{2,1,0:T(8,128)(2,1)} %we_ref.1, bf16[1,2,2048,4096]{3,2,1,0:T(8,128)(2,1)} %wd_ref.1), custom_call_target="tpu_custom_call" | custom-call | flops 12884901888 | bytes 50331648 | tf_op jit(solution)/shard_map/pallas_call | solution.py:318
  101.4 0.0 copy-done
  101.4 1.5 %fusion = bf16[64,2,2048]{2,0,1:T(8,128)(2,1)S(1)} fusion(f32[2,64,2048]{2,1,0:T(8,128)} %shard_map.73, bf16[64,2,2048]{2,1,0:T(2,128)(2,1)S(1)} %copy-done, f32[2,2048]{1,0:T(2,128)S(1)} %convert_element_type.9), kind=kLoop, calls=%fused_computation.1 | loop fusion | flops 1048576 | bytes 2113536 | tf_op jit(solution)/shard_map/convert_element_type | solution.py:356
  102.9 1.3 %copy.9 = bf16[64,2,2048]{2,1,0:T(2,128)(2,1)} copy(bf16[64,2,2048]{2,0,1:T(8,128)(2,1)S(1)} %fusion) | data formatting | bytes 1048576 | tf_op jit(solution)/shard_map/convert_element_type | solution.py:356
Async XLA Ops:
  0.0 101.4 %copy-start = (bf16[64,2,2048]{2,1,0:T(2,128)(2,1)S(1)}, bf16[64,2,2048]{2,1,0:T(2,128)(2,1)}, u32[]{:S(2)}) copy-start(bf16[64,2,2048]{2,1,0:T(2,128)(2,1)} %param.8) | copy-start | bytes 1572868
